TPU v7x, 32 devices: a whole 2x2x4 slice. The times are simulated.
32 devices in a mesh: dp: 8 (over z, y), seq: 4 (over x, core).
Axes of the slice: x: 2, y: 2, z: 4, core: 2. Of those that a mesh axis runs over, the one named last changes fastest.
Arguments:
- tokens: bfloat16 [32768, 512], P(('dp', 'seq')), may hold values from -6 to 6
- memory: bfloat16 [8192, 512], P(('dp', 'seq')), may hold values from -6 to 6
- lengths: int32 [64], P(('dp', 'seq')), may hold values from 128 to 512
- neighbours: int32 [32768, 4], P(('dp', 'seq')), may hold values from 0 to 1023
- out_grad: bfloat16 [32768, 512], P(('dp', 'seq')), may hold values from -6 to 6
- gain_one: bfloat16 [512], P(('dp', 'seq')), may hold values from 0.5 to 1.5
- gain_two: bfloat16 [512], P(('dp', 'seq')), may hold values from 0.5 to 1.5
- w_query: bfloat16 [512, 512], P(('dp', 'seq')), may hold values from -0.5 to 0.5
- w_key: bfloat16 [512, 512], P(('dp', 'seq')), may hold values from -0.25 to 0.25
- w_value: bfloat16 [512, 512], P(('dp', 'seq')), may hold values from -0.25 to 0.25
- w_gate: bfloat16 [512, 8], P(('dp', 'seq')), may hold values from -0.25 to 0.25
- w_out: bfloat16 [512, 512], P(('dp', 'seq')), may hold values from -0.5 to 0.5
- w_up: bfloat16 [512, 2048], P(('dp', 'seq')), may hold values from -0.25 to 0.25
- w_down: bfloat16 [2048, 512], P(('dp', 'seq')), may hold values from -0.125 to 0.125
Outputs:
- block_out: bfloat16 [32768, 512], P(('dp', 'seq'))
- grad_tokens: float32 [32768, 512], P(('dp', 'seq'))
- grad_gain_one: float32 [512], P(('dp', 'seq'))
- grad_gain_two: float32 [512], P(('dp', 'seq'))
- grad_w_query: float32 [512, 512], P(('dp', 'seq'))
- grad_w_key: float32 [512, 512], P(('dp', 'seq'))
- grad_w_value: float32 [512, 512], P(('dp', 'seq'))
- grad_w_gate: float32 [512, 8], P(('dp', 'seq'))
- grad_w_out: float32 [512, 512], P(('dp', 'seq'))
- grad_w_up: float32 [512, 2048], P(('dp', 'seq'))
- grad_w_down: float32 [2048, 512], P(('dp', 'seq'))
Inputs may be any that keep to these rules, and one draw needn't show every extreme that they name: `neighbours`: A token's neighbour ids number the memory states of its own group.
All inputs are finite; a program needn't handle non-finite values.
Results may differ from a plain program's by a relative error of at most 0.013.
The roundings to bfloat16 on the way count: a program that leaves them out, or rounds other values in their place, can miss the bound.
Values may be sent and summed in bfloat16 or wider, within the bound.
No kernel may reach another device: no remote copies, remote signals or barrier semaphores. Data moves between devices by JAX's collectives and lax.ppermute only.
A program may use at most 192 MiB of HBM per device.

v0:
```python
import jax
import jax.numpy as jnp
from jax import lax
from jax.sharding import PartitionSpec as P

EPSILON = 1e-06
MASKED = -1e30


def product(left, right):
    return jnp.dot(left, right, preferred_element_type=jnp.float32)


def against(left, right):
    return lax.dot_general(
        left, right, (((1,), (1,)), ((), ())), preferred_element_type=jnp.float32
    )


def cross(left, right):
    return lax.dot_general(
        left, right, (((0,), (0,)), ((), ())), preferred_element_type=jnp.float32
    )


def cross_exact(left, right):
    return lax.dot_general(
        left,
        right,
        (((0,), (0,)), ((), ())),
        precision=lax.Precision.HIGHEST,
        preferred_element_type=jnp.float32,
    )


def smooth_act(values):
    return jax.nn.gelu(values, approximate=True)


def split_heads(array, groups, heads):
    lead = array.shape[0] // groups
    return array.reshape(groups, lead, heads, -1).transpose(2, 0, 1, 3)


def merge_heads(array):
    heads, groups, lead, size = array.shape
    return array.transpose(1, 2, 0, 3).reshape(groups * lead, heads * size)


def fetch_weights(shards):
    return (
        lax.all_gather(shards[0], ("dp", "seq"), axis=0, tiled=True),
        lax.all_gather(shards[1], ("dp", "seq"), axis=0, tiled=True),
        lax.all_gather(shards[2], ("dp", "seq"), axis=0, tiled=True),
        lax.all_gather(shards[3], ("dp", "seq"), axis=0, tiled=True),
        lax.all_gather(shards[4], ("dp", "seq"), axis=0, tiled=True),
        lax.all_gather(shards[5], ("dp", "seq"), axis=0, tiled=True),
        lax.all_gather(shards[6], ("dp", "seq"), axis=0, tiled=True),
        lax.all_gather(shards[7], ("dp", "seq"), axis=0, tiled=True),
        lax.all_gather(shards[8], ("dp", "seq"), axis=0, tiled=True),
    )


def reduce_grads(terms):
    return (
        lax.psum_scatter(terms[0], ("dp", "seq"), scatter_dimension=0, tiled=True),
        lax.psum_scatter(terms[1], ("dp", "seq"), scatter_dimension=0, tiled=True),
        lax.psum_scatter(terms[2], ("dp", "seq"), scatter_dimension=0, tiled=True),
        lax.psum_scatter(terms[3], ("dp", "seq"), scatter_dimension=0, tiled=True),
        lax.psum_scatter(terms[4], ("dp", "seq"), scatter_dimension=0, tiled=True),
        lax.psum_scatter(terms[5], ("dp", "seq"), scatter_dimension=0, tiled=True),
        lax.psum_scatter(terms[6], ("dp", "seq"), scatter_dimension=0, tiled=True),
        lax.psum_scatter(terms[7], ("dp", "seq"), scatter_dimension=0, tiled=True),
        lax.psum_scatter(terms[8], ("dp", "seq"), scatter_dimension=0, tiled=True),
    )


def on_device(
    tokens,
    memory,
    lengths,
    neighbours,
    out_grad,
    gain_one,
    gain_two,
    w_query,
    w_key,
    w_value,
    w_gate,
    w_out,
    w_up,
    w_down,
):
    shards = (gain_one, gain_two, w_query, w_key, w_value, w_gate, w_out, w_up, w_down)
    (
        gain_first,
        gain_second,
        query_full,
        key_full,
        value_full,
        gate_full,
        outw_full,
        up_full,
        down_full,
    ) = fetch_weights(shards)
    rows, width = tokens.shape
    heads = gate_full.shape[1]
    head_size = width // heads
    seg_count = lengths.shape[0]
    seg_len = rows // seg_count
    knn_count = neighbours.shape[1]
    score_scale = head_size ** (-0.5)
    inputs = tokens.astype(jnp.float32)
    inv_one = lax.rsqrt(jnp.mean(inputs * inputs, axis=-1, keepdims=True) + EPSILON)
    unit_one = inputs * inv_one
    normed = (unit_one * gain_first.astype(jnp.float32)).astype(jnp.bfloat16)
    queries = product(normed, query_full).astype(jnp.bfloat16)
    keys_own = product(normed, key_full).astype(jnp.bfloat16)
    values_own = product(normed, value_full).astype(jnp.bfloat16)
    gate = jax.nn.sigmoid(product(normed, gate_full))
    mem_keys = product(memory, key_full).astype(jnp.bfloat16)
    mem_values = product(memory, value_full).astype(jnp.bfloat16)
    all_keys, all_values = (
        lax.all_gather(mem_keys, "seq", axis=0, tiled=True),
        lax.all_gather(mem_values, "seq", axis=0, tiled=True),
    )
    mem_rows = all_keys.shape[0]
    position = jnp.arange(seg_len)
    allowed = (position[None, None, :] <= position[None, :, None]) & (
        position[None, None, :] < lengths[:, None, None]
    )
    query_head_rows = split_heads(queries, seg_count, heads)
    key_heads = split_heads(keys_own, seg_count, heads)
    value_heads = split_heads(values_own, seg_count, heads)
    memory_key_heads = all_keys.reshape(mem_rows, heads, head_size).transpose(1, 0, 2)
    memory_value_heads = all_values.reshape(mem_rows, heads, head_size).transpose(1, 0, 2)

    def head_scores(query_h, key_h, mkey_h):
        memory_scores = (
            jnp.einsum("sqd,md->sqm", query_h, mkey_h, preferred_element_type=jnp.float32)
            * score_scale
        )
        score_loc = (
            jnp.einsum("sqd,skd->sqk", query_h, key_h, preferred_element_type=jnp.float32)
            * score_scale
        )
        return (memory_scores, jnp.where(allowed, score_loc, MASKED))

    def attend(items):
        query_h, key_h, value_h, mkey_h, mvalue_h = items
        memory_scores, score_loc = head_scores(query_h, key_h, mkey_h)
        peak = jnp.maximum(jnp.max(memory_scores, axis=-1), jnp.max(score_loc, axis=-1))[..., None]
        exp_mem = jnp.exp(memory_scores - peak)
        exp_loc = jnp.exp(score_loc - peak)
        total = jnp.sum(exp_mem, axis=-1, keepdims=True) + jnp.sum(exp_loc, axis=-1, keepdims=True)
        weight_mem = (exp_mem / total).astype(jnp.bfloat16)
        weight_loc = (exp_loc / total).astype(jnp.bfloat16)
        context_h = jnp.einsum(
            "sqm,md->sqd", weight_mem, mvalue_h, preferred_element_type=jnp.float32
        )
        context_h = context_h + jnp.einsum(
            "sqk,skd->sqd", weight_loc, value_h, preferred_element_type=jnp.float32
        )
        return (context_h, peak + jnp.log(total))

    context_heads, log_totals = lax.map(
        attend, (query_head_rows, key_heads, value_heads, memory_key_heads, memory_value_heads)
    )
    context_output = merge_heads(context_heads).reshape(rows, heads, head_size)
    flat_ids = neighbours.reshape(-1)
    near_keys = jnp.take(all_keys, flat_ids, axis=0).reshape(rows, knn_count, heads, head_size)
    near_values = jnp.take(all_values, flat_ids, axis=0).reshape(rows, knn_count, heads, head_size)
    query_rows = queries.reshape(rows, heads, head_size)
    near_scores = (
        jnp.einsum("nhd,njhd->njh", query_rows, near_keys, preferred_element_type=jnp.float32)
        * score_scale
    )
    near_probs = jax.nn.softmax(near_scores, axis=1)
    near_values_f = near_values.astype(jnp.float32)
    recalled = jnp.sum(near_probs[..., None] * near_values_f, axis=1)
    gate_w = gate[:, :, None]
    blend = (1.0 - gate_w) * context_output + gate_w * recalled
    mixed = blend.reshape(rows, width).astype(jnp.bfloat16)
    hidden = inputs + product(mixed, outw_full)
    inv_two = lax.rsqrt(jnp.mean(hidden * hidden, axis=-1, keepdims=True) + EPSILON)
    unit_two = hidden * inv_two
    normed_two = (unit_two * gain_second.astype(jnp.float32)).astype(jnp.bfloat16)
    pre_act = product(normed_two, up_full)
    activated = smooth_act(pre_act).astype(jnp.bfloat16)
    result = hidden + product(activated, down_full)
    back_full = fetch_weights(shards)
    (
        gain_one_back,
        gain_two_back,
        query_back,
        key_back,
        value_back,
        gate_back,
        outw_back,
        up_back,
        down_back,
    ) = back_full
    grad_down = cross(activated, out_grad)
    grad_act = against(out_grad, down_back)
    pre_back = product(normed_two, up_back)
    _, gelu_pull = jax.vjp(smooth_act, pre_back)
    grad_pre = gelu_pull(grad_act)[0].astype(jnp.bfloat16)
    grad_up = cross(normed_two, grad_pre)
    grad_normed_two = against(grad_pre, up_back)
    grad_gain_two = jnp.sum(grad_normed_two * unit_two, axis=0)
    grad_unit_two = grad_normed_two * gain_two_back.astype(jnp.float32)
    grad_hidden = out_grad.astype(jnp.float32) + inv_two * (
        grad_unit_two - unit_two * jnp.mean(grad_unit_two * unit_two, axis=-1, keepdims=True)
    )
    grad_branch = grad_hidden.astype(jnp.bfloat16)
    grad_outw = cross(mixed, grad_branch)
    grad_mixed = against(grad_branch, outw_back).reshape(rows, heads, head_size)
    grad_context = ((1.0 - gate_w) * grad_mixed).astype(jnp.bfloat16)
    grad_recalled = gate_w * grad_mixed
    grad_gate_val = jnp.sum(grad_mixed * (recalled - context_output), axis=-1)
    grad_logit = (grad_gate_val * gate * (1.0 - gate)).astype(jnp.bfloat16)
    grad_near_probs = jnp.sum(grad_recalled[:, None] * near_values_f, axis=-1)
    grad_near_values = near_probs[..., None] * grad_recalled[:, None]
    grad_near_scores = near_probs * (
        grad_near_probs - jnp.sum(near_probs * grad_near_probs, axis=1, keepdims=True)
    )
    grad_query_near = score_scale * jnp.sum(
        grad_near_scores[..., None] * near_keys.astype(jnp.float32), axis=1
    )
    grad_near_keys = (
        score_scale * grad_near_scores[..., None] * query_rows.astype(jnp.float32)[:, None]
    )
    near_key_sum = jax.ops.segment_sum(
        grad_near_keys.reshape(rows * knn_count, width), flat_ids, num_segments=mem_rows
    )
    near_value_sum = jax.ops.segment_sum(
        grad_near_values.reshape(rows * knn_count, width), flat_ids, num_segments=mem_rows
    )
    grad_context_heads = split_heads(grad_context.reshape(rows, width), seg_count, heads)

    def attend_back(items):
        query_h, key_h, value_h, mkey_h, mvalue_h, log_h, dctx_h = items
        memory_scores, score_loc = head_scores(query_h, key_h, mkey_h)
        prob_mem = jnp.exp(memory_scores - log_h)
        prob_loc = jnp.exp(score_loc - log_h)
        dprob_mem = jnp.einsum("sqd,md->sqm", dctx_h, mvalue_h, preferred_element_type=jnp.float32)
        dprob_loc = jnp.einsum("sqd,skd->sqk", dctx_h, value_h, preferred_element_type=jnp.float32)
        row_total = jnp.sum(prob_mem * dprob_mem, axis=-1, keepdims=True) + jnp.sum(
            prob_loc * dprob_loc, axis=-1, keepdims=True
        )
        dscore_mem = (prob_mem * (dprob_mem - row_total)).astype(jnp.bfloat16)
        dscore_loc = (prob_loc * (dprob_loc - row_total)).astype(jnp.bfloat16)
        dquery = jnp.einsum("sqm,md->sqd", dscore_mem, mkey_h, preferred_element_type=jnp.float32)
        dquery = score_scale * (
            dquery
            + jnp.einsum("sqk,skd->sqd", dscore_loc, key_h, preferred_element_type=jnp.float32)
        )
        dkey = score_scale * jnp.einsum(
            "sqk,sqd->skd", dscore_loc, query_h, preferred_element_type=jnp.float32
        )
        dvalue = jnp.einsum(
            "sqk,sqd->skd",
            prob_loc.astype(jnp.bfloat16),
            dctx_h,
            preferred_element_type=jnp.float32,
        )
        dmkey = score_scale * jnp.einsum(
            "sqm,sqd->md", dscore_mem, query_h, preferred_element_type=jnp.float32
        )
        dmvalue = jnp.einsum(
            "sqm,sqd->md", prob_mem.astype(jnp.bfloat16), dctx_h, preferred_element_type=jnp.float32
        )
        return (dquery, dkey, dvalue, dmkey, dmvalue)

    dquery_heads, dkey_heads, dvalue_heads, dmkey_heads, dmvalue_heads = lax.map(
        attend_back,
        (
            query_head_rows,
            key_heads,
            value_heads,
            memory_key_heads,
            memory_value_heads,
            log_totals,
            grad_context_heads,
        ),
    )
    grad_queries = (merge_heads(dquery_heads) + grad_query_near.reshape(rows, width)).astype(
        jnp.bfloat16
    )
    grad_keys = merge_heads(dkey_heads).astype(jnp.bfloat16)
    grad_values = merge_heads(dvalue_heads).astype(jnp.bfloat16)
    mem_grad_keys = merge_heads(dmkey_heads[:, None]) + near_key_sum
    mem_grad_values = merge_heads(dmvalue_heads[:, None]) + near_value_sum
    own_key_grad, own_value_grad = (
        lax.psum_scatter(
            mem_grad_keys.astype(jnp.bfloat16), "seq", scatter_dimension=0, tiled=True
        ).astype(jnp.float32),
        lax.psum_scatter(
            mem_grad_values.astype(jnp.bfloat16), "seq", scatter_dimension=0, tiled=True
        ).astype(jnp.float32),
    )
    memory_f = memory.astype(jnp.float32)
    key_mem_term = cross_exact(memory_f, own_key_grad)
    value_mem_term = cross_exact(memory_f, own_value_grad)
    grad_query = cross(normed, grad_queries)
    grad_key = cross(normed, grad_keys) + key_mem_term
    grad_value = cross(normed, grad_values) + value_mem_term
    grad_gate = cross(normed, grad_logit)
    grad_normed = against(grad_queries, query_back) + against(grad_keys, key_back)
    grad_normed = grad_normed + against(grad_values, value_back) + against(grad_logit, gate_back)
    grad_gain_one = jnp.sum(grad_normed * unit_one, axis=0)
    grad_unit_one = grad_normed * gain_one_back.astype(jnp.float32)
    grad_inputs = grad_hidden + inv_one * (
        grad_unit_one - unit_one * jnp.mean(grad_unit_one * unit_one, axis=-1, keepdims=True)
    )
    summed = reduce_grads(
        (
            grad_gain_one,
            grad_gain_two,
            grad_query,
            grad_key,
            grad_value,
            grad_gate,
            grad_outw,
            grad_up,
            grad_down,
        )
    )
    return (
        result.astype(jnp.bfloat16),
        grad_inputs,
        summed[0],
        summed[1],
        summed[2],
        summed[3],
        summed[4],
        summed[5],
        summed[6],
        summed[7],
        summed[8],
    )


def solution(mesh):
    in_specs = (
        P(("dp", "seq"), None),
        P(("dp", "seq"), None),
        P(("dp", "seq")),
        P(("dp", "seq"), None),
        P(("dp", "seq"), None),
        P(("dp", "seq")),
        P(("dp", "seq")),
        P(("dp", "seq"), None),
        P(("dp", "seq"), None),
        P(("dp", "seq"), None),
        P(("dp", "seq"), None),
        P(("dp", "seq"), None),
        P(("dp", "seq"), None),
        P(("dp", "seq"), None),
    )
    out_specs = (
        P(("dp", "seq"), None),
        P(("dp", "seq"), None),
        P(("dp", "seq")),
        P(("dp", "seq")),
        P(("dp", "seq"), None),
        P(("dp", "seq"), None),
        P(("dp", "seq"), None),
        P(("dp", "seq"), None),
        P(("dp", "seq"), None),
        P(("dp", "seq"), None),
        P(("dp", "seq"), None),
    )
    return jax.shard_map(
        on_device, mesh=mesh, in_specs=in_specs, out_specs=out_specs, check_vma=False
    )
```

profile of v0, /device:TPU:0, one launch (start us, length us, event | category | flops | bytes accessed | tf_op | source)
XLA Modules:
  0.0 1761.5 jit_solution(10807271396962826313)
XLA Ops:
  7.2 45.0 %all_gather.45 = bf16[512,512]{1,0:T(8,128)(2,1)S(1)} all-gather(bf16[16,512]{1,0:T(8,128)(2,1)} %param.28), channel_id=1, replica_groups=mesh['dp'=8,'seq'=4] {'dp','seq'}, dimensions={0}, use_global_device_ids=true | all-gather | bytes 540672 | tf_op jit(solution)/shard_map/all_gather | solution.py:55
  53.4 38.4 %all_gather.47 = bf16[512,512]{1,0:T(8,128)(2,1)S(1)} all-gather(bf16[16,512]{1,0:T(8,128)(2,1)} %param.29), channel_id=1, replica_groups=mesh['dp'=8,'seq'=4] {'dp','seq'}, dimensions={0}, use_global_device_ids=true | all-gather | bytes 540672 | tf_op jit(solution)/shard_map/all_gather | solution.py:56
  95.5 37.0 %all-reduce.5 = (bf16[512]{0:T(512)(128)(2,1)S(1)}, bf16[512]{0:T(512)(128)(2,1)S(1)}) all-reduce(bf16[512]{0:T(512)(128)(2,1)S(1)} %dynamic-update-slice, bf16[512]{0:T(512)(128)(2,1)S(1)} %dynamic-update-slice.1), channel_id=1, replica_groups=mesh['dp'=8,'seq'=4] {'dp','seq'}, use_global_device_ids=true, to_apply=%add | all-reduce | flops 1024 | bytes 4096
  149.6 42.9 %all_gather.44 = bf16[512,512]{1,0:T(8,128)(2,1)S(1)} all-gather(bf16[16,512]{1,0:T(8,128)(2,1)S(1)} %copy-done.54), channel_id=1, replica_groups=mesh['dp'=8,'seq'=4] {'dp','seq'}, dimensions={0}, use_global_device_ids=true | all-gather | bytes 540672 | tf_op jit(solution)/shard_map/all_gather | solution.py:54
  200.8 37.0 %all-gather = bf16[32,16,8]{1,2,0:T(8,128)(2,1)S(1)} all-gather(bf16[1,16,8]{1,2,0:T(8,128)(2,1)S(1)} %bitcast.343), channel_id=1, replica_groups=mesh['dp'=8,'seq'=4] {'dp','seq'}, dimensions={0}, use_global_device_ids=true | all-gather | bytes 8448 | tf_op jit(solution)/shard_map/all_gather | solution.py:57
  238.5 42.5 %all_gather.49 = bf16[512,512]{1,0:T(8,128)(2,1)} all-gather(bf16[16,512]{1,0:T(8,128)(2,1)S(1)} %copy-done.55), channel_id=1, replica_groups=mesh['dp'=8,'seq'=4] {'dp','seq'}, dimensions={0}, use_global_device_ids=true | all-gather | bytes 540672 | tf_op jit(solution)/shard_map/all_gather | solution.py:58
  288.7 71.1 %while.32 = (s32[]{:T(128)}, f32[8,2,512,64]{2,3,1,0:T(8,128)S(1)}, f32[8,2,512,1]{2,1,3,0:T(2,128)}, bf16[8,2,512,64]{2,3,1,0:T(8,128)(2,1)}, bf16[8,1024,64]{1...) while((s32[]{:T(128)}, f32[8,2,512,64]{2,3,1,0:T(8,128)S(1)}, ...), condition=%wide.region_6.7_spmd.clone, body=%wide.region_1.6_spmd.clone.sunk | while | flops 416873472 | bytes 20788332 | solution.py:166
  363.3 17.4 gather_fusion
  380.7 17.3 gather_fusion.1
  504.5 21.0 %broadcast_multiply_fusion.1 = (f32[1024,4,8,64]{3,2,1,0:T(8,128)}, f32[1024,4,8]{2,1,0:T(4,128)}) fusion(f32[1024,8,64]{2,1,0:T(8,128)} %copy.287, f32[1024,4,8]{2,1,0:T(4,128)S(1)} %copy-done.20, f32[1024,4,8,64]{3,2,1,0:T(8,128)} %reshape.243), kind=kLoop, calls=%fused_computation.121 | loop fusion | flops 6258688 | bytes 19136512 | tf_op jit(solution)/shard_map/mul | solution.py:223
  525.6 14.2 reshape.272
  543.5 144.8 %while.33 = (s32[]{:T(128)}, f32[8,2,512,64]{2,3,1,0:T(8,128)}, bf16[8,2,512,64]{2,3,1,0:T(8,128)(2,1)}, bf16[8,2,512,64]{2,3,1,0:T(8,128)(2,1)}, f32[8,1024,64]...) while((s32[]{:T(128)}, f32[8,2,512,64]{2,3,1,0:T(8,128)}, ...), condition=%wide.region_15.17_spmd.clone, body=%wide.region_12.16_spmd.clone.sunk | while | flops 1024719872 | bytes 51183256 | solution.py:275
  690.2 26.0 %scatter_fusion.1 = f32[1024,512]{1,0:T(8,128)S(1)} fusion(f32[1024,512]{1,0:T(8,128)S(1)} %copy.303, s32[4096]{0:T(1024)S(1)} %copy-done.38, f32[4096,512]{1,0:T(8,128)} %reshape.272), kind=kCustom, calls=%fused_computation.3 | custom fusion | flops 2097152 | bytes 25182208 | tf_op jit(solution)/shard_map/scatter-add | solution.py:236
  723.0 17.2 multiply_reduce_fusion.4
  740.2 14.2 reshape.264
  756.4 26.0 %scatter_fusion = f32[1024,512]{1,0:T(8,128)S(1)} fusion(f32[1024,512]{1,0:T(8,128)S(1)} %copy.301, s32[4096]{0:T(1024)S(1)} %copy-done.38, f32[4096,512]{1,0:T(8,128)} %reshape.264), kind=kCustom, calls=%fused_computation.2 | custom fusion | flops 2097152 | bytes 25182208 | tf_op jit(solution)/shard_map/scatter-add | solution.py:233
  842.6 37.1 %all-reduce.4 = (f32[512]{0:T(512)S(1)}, f32[512]{0:T(512)S(1)}) all-reduce(f32[512]{0:T(512)S(1)} %get-tuple-element.430, f32[512]{0:T(512)S(1)} %copy-done.57), channel_id=2, replica_groups=mesh['dp'=8,'seq'=4] {'dp','seq'}, use_global_device_ids=true, to_apply=%region_22.24.clone | all-reduce | flops 1024 | bytes 8192
  896.2 44.7 %reduce-scatter.28.cloned.1.call-done = f32[16,8]{1,0:T(8,128)} async-done(((f32[512,8]{1,0:T(8,128)}), f32[16,8]{1,0:T(8,128)}) %reduce-scatter.28.cloned.1.call-update) | async-done | bytes 528
  942.2 132.2 %reduce-scatter.12.cloned.1.call-done = f32[16,512]{1,0:T(8,128)} async-done(((f32[512,512]{1,0:T(8,128)}), f32[16,512]{1,0:T(8,128)}) %reduce-scatter.12.cloned.1.call-update) | async-done | bytes 32784 | tf_op jit(solution)/shard_map/reduce_scatter | solution.py:68
  1074.5 133.6 %reduce-scatter.22.cloned.1.call-done = f32[16,512]{1,0:T(8,128)} async-done(((f32[512,512]{1,0:T(8,128)}), f32[16,512]{1,0:T(8,128)}) %reduce-scatter.22.cloned.1.call-update) | async-done | bytes 32784 | tf_op jit(solution)/shard_map/reduce_scatter | solution.py:72
  1208.1 133.5 %reduce-scatter.20.cloned.1.call-done = f32[16,512]{1,0:T(8,128)} async-done(((f32[512,512]{1,0:T(8,128)}), f32[16,512]{1,0:T(8,128)}) %reduce-scatter.20.cloned.1.call-update) | async-done | bytes 32784 | tf_op jit(solution)/shard_map/reduce_scatter | solution.py:70
  1341.6 133.6 %reduce-scatter.16.cloned.1.call-done = f32[16,512]{1,0:T(8,128)} async-done(((f32[512,512]{1,0:T(8,128)}), f32[16,512]{1,0:T(8,128)}) %reduce-scatter.16.cloned.1.call-update) | async-done | bytes 32784 | tf_op jit(solution)/shard_map/reduce_scatter | solution.py:69
  1475.2 139.6 %reduce-scatter.24.cloned.1.call-done = f32[16,2048]{1,0:T(8,128)} async-done(((f32[512,2048]{1,0:T(8,128)}), f32[16,2048]{1,0:T(8,128)}) %reduce-scatter.24.cloned.1.call-update) | async-done | bytes 131088 | tf_op jit(solution)/shard_map/reduce_scatter | solution.py:73
  1614.8 139.8 %reduce-scatter.26.cloned.1.call-done = f32[64,512]{1,0:T(8,128)} async-done(((f32[2048,512]{1,0:T(8,128)}), f32[64,512]{1,0:T(8,128)}) %reduce-scatter.26.cloned.1.call-update) | async-done | bytes 131088 | tf_op jit(solution)/shard_map/reduce_scatter | solution.py:74
  (435 shorter events, 455.1 us)
Async XLA Ops:
  7.2 45.1 %copy-start = (bf16[256,512]{1,0:T(8,128)(2,1)S(1)}, bf16[256,512]{1,0:T(8,128)(2,1)}, u32[]{:S(2)}) copy-start(bf16[256,512]{1,0:T(8,128)(2,1)} %param.21) | copy-start | bytes 786436
  7.2 87.0 %copy-start.34 = (bf16[1024,512]{1,0:T(8,128)(2,1)S(1)}, bf16[1024,512]{1,0:T(8,128)(2,1)}, u32[]{:S(2)}) copy-start(bf16[1024,512]{1,0:T(8,128)(2,1)} %param.20) | copy-start | bytes 3145732
  7.2 276.7 %all-gather.6.cloned.1.call-start = ((), (), s32[]{:S(2)}) async-start(), calls=%async_computation.9 | async-start | bytes 1310720 | tf_op jit(solution)/shard_map/all_gather | solution.py:124
  52.3 80.3 %copy-start.21 = (bf16[512,512]{1,0:T(8,128)(2,1)}, bf16[512,512]{1,0:T(8,128)(2,1)S(1)}, u32[]{:S(2)}) copy-start(bf16[512,512]{1,0:T(8,128)(2,1)S(1)} %all_gather.45) | copy-start | bytes 1572868
  53.3 232.9 %all-gather.8.cloned.1.call-start = ((), (), s32[]{:S(2)}) async-start(), calls=%async_computation.10 | async-start | bytes 1310720 | tf_op jit(solution)/shard_map/all_gather | solution.py:125
  92.8 376.1 %all-gather.10.cloned.1.call-start = ((), (), s32[]{:S(2)}) async-start(), calls=%async_computation.11 | async-start | bytes 2162688 | tf_op jit(solution)/shard_map/all_gather | solution.py:59
  93.6 383.4 %all-gather.12.cloned.1.call-start = ((), (), s32[]{:S(2)}) async-start(), calls=%async_computation.12 | async-start | bytes 2162688 | tf_op jit(solution)/shard_map/all_gather | solution.py:60
  94.1 712.0 %reduce-scatter.18.cloned.1.call-start = ((), (), s32[]{:S(2)}) async-start(), calls=%async_computation.16 | async-start | bytes 1310720 | tf_op jit(solution)/shard_map/reduce_scatter | solution.py:298
  94.7 371.5 %copy-start.6 = (bf16[1024,512]{0,1:T(8,128)(2,1)}, bf16[1024,512]{0,1:T(8,128)(2,1)S(1)}, u32[]{:S(2)}) copy-start(bf16[1024,512]{0,1:T(8,128)(2,1)S(1)} %copy.267) | copy-start | bytes 3145732
  95.0 143.0 %copy-start.45 = (f32[1024]{0:T(1024)}, f32[1024]{0:T(1024)S(1)}, u32[]{:S(2)}) copy-start(f32[1024]{0:T(1024)S(1)} %add_rsqrt_fusion.1) | copy-start | bytes 12292
  132.6 105.5 %copy-start.51 = (f32[512]{0:T(512)}, f32[512]{0:T(512)S(1)}, u32[]{:S(2)}) copy-start(f32[512]{0:T(512)S(1)} %convert_element_type.122) | copy-start | bytes 6148
  138.2 144.7 %copy-start.14 = (bf16[8,2,512,64]{2,3,1,0:T(8,128)(2,1)}, bf16[8,2,512,64]{2,3,1,0:T(8,128)(2,1)S(1)}, u32[]{:S(2)}) copy-start(bf16[8,2,512,64]{2,3,1,0:T(8,128)(2,1)S(1)} %fusion.151) | copy-start | bytes 3145732
  200.8 80.1 %copy-start.35 = (bf16[1024,512]{1,0:T(8,128)(2,1)S(1)}, bf16[1024,512]{1,0:T(8,128)(2,1)}, u32[]{:S(2)}) copy-start(bf16[1024,512]{1,0:T(8,128)(2,1)} %param.24) | copy-start | bytes 3145732
  238.1 44.2 %copy-start.49 = (bf16[512,8]{0,1:T(8,128)(2,1)}, bf16[512,8]{0,1:T(8,128)(2,1)S(1)}, u32[]{:S(2)}) copy-start(bf16[512,8]{0,1:T(8,128)(2,1)S(1)} %reshape.285) | copy-start | bytes 24580
  238.5 260.5 %copy-start.39 = (f32[1024,8]{0,1:T(8,128)}, f32[1024,8]{0,1:T(8,128)S(1)}, u32[]{:S(2)}) copy-start(f32[1024,8]{0,1:T(8,128)S(1)} %get-tuple-element.503) | copy-start | bytes 98308
  281.0 209.0 %copy-start.47 = (f32[512]{0:T(512)}, f32[512]{0:T(512)S(1)}, u32[]{:S(2)}) copy-start(f32[512]{0:T(512)S(1)} %convert_element_type.132) | copy-start | bytes 6148
  717.3 96.8 %reduce-scatter.14.cloned.1.call-start = ((), (), s32[]{:S(2)}) async-start(), calls=%async_computation.14 | async-start | bytes 1310720 | tf_op jit(solution)/shard_map/reduce_scatter | solution.py:295
  783.6 157.3 %reduce-scatter.28.cloned.1.call-start = ((), (), s32[]{:S(2)}) async-start(), calls=%async_computation.21 | async-start | bytes 270336
  796.3 278.2 %reduce-scatter.12.cloned.1.call-start = ((), (), s32[]{:S(2)}) async-start(), calls=%async_computation.13 | async-start | bytes 1081344 | tf_op jit(solution)/shard_map/reduce_scatter | solution.py:68
  799.5 408.6 %reduce-scatter.22.cloned.1.call-start = ((), (), s32[]{:S(2)}) async-start(), calls=%async_computation.18 | async-start | bytes 1081344 | tf_op jit(solution)/shard_map/reduce_scatter | solution.py:72
  802.5 539.1 %reduce-scatter.20.cloned.1.call-start = ((), (), s32[]{:S(2)}) async-start(), calls=%async_computation.17 | async-start | bytes 1081344 | tf_op jit(solution)/shard_map/reduce_scatter | solution.py:70
  810.4 664.8 %reduce-scatter.16.cloned.1.call-start = ((), (), s32[]{:S(2)}) async-start(), calls=%async_computation.15 | async-start | bytes 1081344 | tf_op jit(solution)/shard_map/reduce_scatter | solution.py:69
  818.5 796.3 %reduce-scatter.24.cloned.1.call-start = ((), (), s32[]{:S(2)}) async-start(), calls=%async_computation.19 | async-start | bytes 4325376 | tf_op jit(solution)/shard_map/reduce_scatter | solution.py:73
  825.8 928.8 %reduce-scatter.26.cloned.1.call-start = ((), (), s32[]{:S(2)}) async-start(), calls=%async_computation.20 | async-start | bytes 4325376 | tf_op jit(solution)/shard_map/reduce_scatter | solution.py:74
  (51 other events, 263.0 us)
Sparse Core Ops, SparseCore 0:
  53.4 13.1 all-gather.5
  92.9 14.7 all-gather.7
  110.6 56.7 all-gather.9
  170.1 55.3 all-gather.11
  717.5 21.1 reduce-scatter.17
  783.7 21.0 reduce-scatter.13
  807.0 133.8 reduce-scatter.27
  943.8 130.6 reduce-scatter.11
  1077.3 130.7 reduce-scatter.21
  1210.8 130.7 reduce-scatter.19
  1344.4 130.7 reduce-scatter.15
  1478.0 136.7 reduce-scatter.23
  1617.7 136.7 reduce-scatter.25
where the time goes:
time: 1770 us; the launch traced here: 1760 us
  waiting for transfers between devices  858 us (48%)
  blocking collectives  280 us (16%)
  matrix products  258 us (15%)
  local copies, waits for them, and re-layouts  176 us (10%)
  other arithmetic  172 us (10%)
    reduce_scatter x1, waiting for transfers between devices, reduce_grads(): lax.psum_scatter(terms[8], ('dp', 'seq'), scatter_dimension=0, tiled=True)  140 us
    reduce_scatter x1, waiting for transfers between devices, reduce_grads(): lax.psum_scatter(terms[7], ('dp', 'seq'), scatter_dimension=0, tiled=True)  140 us
    reduce_scatter x1, waiting for transfers between devices, reduce_grads(): lax.psum_scatter(terms[6], ('dp', 'seq'), scatter_dimension=0, tiled=True)  134 us
    reduce_scatter x1, waiting for transfers between devices, reduce_grads(): lax.psum_scatter(terms[3], ('dp', 'seq'), scatter_dimension=0, tiled=True)  134 us
    reduce_scatter x1, waiting for transfers between devices, reduce_grads(): lax.psum_scatter(terms[4], ('dp', 'seq'), scatter_dimension=0, tiled=True)  134 us
    reduce_scatter x1, waiting for transfers between devices, reduce_grads(): lax.psum_scatter(terms[2], ('dp', 'seq'), scatter_dimension=0, tiled=True)  132 us
    unnamed x2, blocking collectives  74.2 us
    unnamed x14, waiting for transfers between devices  46.1 us
  transfers between devices with their start and end apart: 13, of which 7 were waited for; matrix products, arithmetic and copies ran while one was open for 20% of the time, Pallas kernels for 0%

commit v1 on v0

v1 whole, which is shorter than its diff:
```python
import functools
import math

import jax
import jax.numpy as jnp
from jax import lax
from jax.experimental import pallas as pl
from jax.experimental.pallas import tpu as pltpu
from jax.sharding import PartitionSpec as P


EPSILON = 1e-06
MASKED = -1e30
LOG2E = math.log2(math.e)
F32 = jnp.float32
BF16 = jnp.bfloat16
VMEM_BYTES = 58 << 20
SIDE = 128
TILE = 256


def dot(left, right, left_dim=1, right_dim=0):
    return lax.dot_general(
        left, right, (((left_dim,), (right_dim,)), ((), ())), preferred_element_type=F32
    )


def call(kernel, outs, grid=None, in_specs=None, out_specs=None, scratch=(), flops=0, byte_count=0):
    options = {}
    if grid is not None:
        options = dict(grid=grid, in_specs=in_specs, out_specs=out_specs)
    return pl.pallas_call(
        kernel,
        out_shape=[jax.ShapeDtypeStruct(shape, kind) for shape, kind in outs],
        scratch_shapes=list(scratch),
        compiler_params=pltpu.CompilerParams(vmem_limit_bytes=VMEM_BYTES),
        cost_estimate=pl.CostEstimate(flops=flops, bytes_accessed=byte_count, transcendentals=0),
        **options,
    )


def whole(shape):
    zeros = (0,) * len(shape)
    return pl.BlockSpec(shape, lambda *_: zeros)


def three_parts(value):
    high = value.astype(BF16).astype(F32)
    rest = value - high
    middle = rest.astype(BF16).astype(F32)
    return high, middle, rest - middle


def pick_rows(rows, count):
    shape = (count, rows[0].shape[1])
    index = lax.broadcasted_iota(jnp.int32, shape, 0)
    block = jnp.zeros(shape, F32)
    for at, row in enumerate(rows):
        block = jnp.where(index == at, row, block)
    return block


def bits_of(size):
    return [1 << b for b in range(size.bit_length() - 1)]


def gather_steps(sizes):
    return [("dp", bit) for bit in reversed(bits_of(sizes["dp"]))] + [
        ("seq", bit) for bit in reversed(bits_of(sizes["seq"]))
    ]


def swap(array, step, sizes):
    axis, bit = step
    return lax.ppermute(array, axis, [(i, i ^ bit) for i in range(sizes[axis])])


def doubled(array, steps, sizes):
    for step in steps:
        array = jnp.concatenate([array, swap(array, step, sizes)], axis=0)
    return array


def halved(array, steps, sizes):
    for step in reversed(steps):
        half = array.shape[0] // 2
        other = swap(array[half:], step, sizes)
        array = array[:half].astype(F32) + other.astype(F32)
        if half > 1:
            array = array.astype(BF16)
    return array[0]


def places(steps, sizes):
    n_seq = sizes["seq"]
    ids = jnp.arange(sizes["dp"] * n_seq, dtype=jnp.int32)
    apart = {"dp": (ids // n_seq) ^ lax.axis_index("dp"), "seq": (ids % n_seq) ^ lax.axis_index("seq")}
    place = jnp.zeros_like(ids)
    for at, (axis, bit) in enumerate(steps):
        place = place | jnp.where((apart[axis] & bit) != 0, 1 << at, 0)
    return place


def owners(steps, sizes):
    n_seq = sizes["seq"]
    at = jnp.arange(sizes["dp"] * n_seq, dtype=jnp.int32)
    own = {"dp": lax.axis_index("dp"), "seq": lax.axis_index("seq")}
    for number, (axis, bit) in enumerate(steps):
        own[axis] = own[axis] ^ jnp.where((at >> number) & 1, bit, 0)
    return own["dp"] * n_seq + own["seq"]


def prepare_kernel(x_ref, g_ref, ids_ref, xt_ref, gt_ref, inv_ref, bias_ref, *, count):
    xt = x_ref[...].astype(F32).T
    xt_ref[...] = xt.astype(BF16)
    gt_ref[...] = g_ref[...].astype(F32).T.astype(BF16)
    inv = lax.rsqrt(jnp.mean(xt * xt, axis=0, keepdims=True) + EPSILON)
    inv_ref[...] = jnp.broadcast_to(inv, inv_ref.shape)
    slots, rows = bias_ref.shape
    step = 128

    def body(i, _):
        at = pl.multiple_of(i * step, step)
        slot = lax.broadcasted_iota(jnp.int32, (step, rows), 0) + at
        times = jnp.zeros((step, rows), F32)
        for j in range(count):
            times = times + jnp.where(ids_ref[j : j + 1, :] == slot, 1.0, 0.0)
        bias_ref[pl.ds(at, step), :] = jnp.where(times > 0.0, jnp.log2(times), MASKED)
        return 0

    lax.fori_loop(0, slots // step, body, 0)


def project_kernel(xt_ref, inv_ref, w_ref, memory_ref, nt_ref, qkv_ref, mem_ref, gate_ref):
    width = xt_ref.shape[0]
    gain = w_ref[:, 3 * width :].astype(F32)[:, 8:9]
    normed = (xt_ref[...].astype(F32) * inv_ref[0:1, :] * gain).astype(BF16)
    nt_ref[...] = normed
    for part in range(3):
        qkv_ref[part * width : (part + 1) * width, :] = dot(
            w_ref[:, part * width : (part + 1) * width], normed, 0, 0
        ).astype(BF16)
    logit = dot(w_ref[:, 3 * width :], normed, 0, 0)
    gate_ref[...] = jax.nn.sigmoid(logit[0:8])
    for part in range(2):
        mem_ref[part * width : (part + 1) * width, :] = dot(
            w_ref[:, (part + 1) * width : (part + 2) * width], memory_ref[...], 0, 1
        ).astype(BF16)


def local_penalty(lengths_ref, rows, seg_count):
    seg_len = rows // seg_count
    lane = lax.broadcasted_iota(jnp.int32, (1, rows), 1)
    last = jnp.zeros((1, rows), jnp.int32)
    for seg in range(seg_count):
        last = jnp.where(lane // seg_len == seg, seg * seg_len + lengths_ref[seg], last)
    return jnp.where(lane < last, 0.0, MASKED)


def causal_bias(size):
    key = lax.broadcasted_iota(jnp.int32, (size, size), 0)
    query = lax.broadcasted_iota(jnp.int32, (size, size), 1)
    return jnp.where(key <= query, 0.0, MASKED)


def attend_kernel(
    lengths_ref, q_ref, k_ref, v_ref, mk_ref, mv_ref, gate_ref, bias_ref,
    mixed_ref, ctx_ref, rec_ref, lse_ref, lsen_ref,
    *, seg_count, scale,
):
    head = pl.program_id(0)
    size, rows = q_ref.shape
    seg_len = rows // seg_count
    penalty = local_penalty(lengths_ref, rows, seg_count)
    causal = causal_bias(TILE)
    q = q_ref[...].astype(F32) * (scale * LOG2E)
    q_high = q.astype(BF16)
    q_low = (q - q_high.astype(F32)).astype(BF16)
    queries = jnp.concatenate([q_high, q_low, jnp.ones((16, rows), BF16)], axis=0)
    keys = jnp.concatenate([k_ref[...], k_ref[...], pick_rows([penalty], 16).astype(BF16)], axis=0)
    mem_keys = jnp.concatenate([mk_ref[...], mk_ref[...]], axis=0)
    values = jnp.concatenate([v_ref[...], jnp.ones((16, rows), BF16)], axis=0)
    mem_values = jnp.concatenate([mv_ref[...], jnp.ones((16, mk_ref.shape[1]), BF16)], axis=0)
    gate = gate_ref[pl.ds(head, 1), :]
    for at in range(0, rows, TILE):
        here = slice(at, at + TILE)
        start = at // seg_len * seg_len
        score_mem = dot(mem_keys, queries[: 2 * size, here], 0, 0)
        score_loc = dot(keys[:, start : at + TILE], queries[:, here], 0, 0)
        diagonal = score_loc[at - start :] + causal
        peak = jnp.maximum(
            jnp.max(score_mem, axis=0, keepdims=True), jnp.max(diagonal, axis=0, keepdims=True)
        )
        if at > start:
            peak = jnp.maximum(peak, jnp.max(score_loc[: at - start], axis=0, keepdims=True))
        near = score_mem + bias_ref[:, here]
        near_peak = jnp.max(near, axis=0, keepdims=True)
        exp_mem = jnp.exp2(score_mem - peak).astype(BF16)
        total = dot(mem_values, exp_mem)
        exp_diag = jnp.exp2(diagonal - peak).astype(BF16)
        total = total + dot(values[:, at : at + TILE], exp_diag)
        if at > start:
            exp_loc = jnp.exp2(score_loc[: at - start] - peak).astype(BF16)
            total = total + dot(values[:, start:at], exp_loc)
        exp_near = jnp.exp2(near - near_peak).astype(BF16)
        near_total = dot(mem_values, exp_near)
        context = total[:size] / total[size : size + 1]
        recalled = near_total[:size] / near_total[size : size + 1]
        ctx_ref[:, here] = context
        rec_ref[:, here] = recalled
        lse_ref[pl.ds(head, 1), here] = peak + jnp.log2(total[size : size + 1])
        lsen_ref[pl.ds(head, 1), here] = near_peak + jnp.log2(near_total[size : size + 1])
        share = gate[:, here]
        mixed_ref[:, here] = ((1.0 - share) * context + share * recalled).astype(BF16)


def feed_kernel(
    xt_ref, gt_ref, mixed_ref, ctx_ref, rec_ref, gate_ref, gain_ref, wo_ref, up_ref, down_ref,
    block_ref, gh_ref, dm_ref, dc_ref, dn_ref, dlogit_ref, ggain_ref, gwo_ref, gup_ref, gdown_ref,
    hidden_ref, n2_ref, out_ref, gn2_ref,
    *, heads,
):
    step = pl.program_id(0)
    last = pl.num_programs(0) - 1
    width, rows = xt_ref.shape
    gain = gain_ref[...].astype(F32)[:, 9:10]

    @pl.when(step == 0)
    def _():
        hidden = xt_ref[...].astype(F32) + dot(wo_ref[...], mixed_ref[...], 0, 0)
        hidden_ref[...] = hidden
        inv = lax.rsqrt(jnp.mean(hidden * hidden, axis=0, keepdims=True) + EPSILON)
        n2_ref[...] = (hidden * inv * gain).astype(BF16)
        out_ref[...] = jnp.zeros_like(out_ref)
        gn2_ref[...] = jnp.zeros_like(gn2_ref)

    n2 = n2_ref[...]
    grad = gt_ref[...]
    pre = dot(up_ref[...], n2, 0, 0)
    coef = math.sqrt(2.0 / math.pi)
    square = pre * pre
    tanh = jnp.tanh(coef * pre * (1.0 + 0.044715 * square))
    half = 0.5 * (1.0 + tanh)
    act = (pre * half).astype(BF16)
    slope = half + 0.5 * coef * pre * (1.0 - tanh * tanh) * (1.0 + (3.0 * 0.044715) * square)
    grad_pre = (dot(down_ref[...], grad) * slope).astype(BF16)
    out_ref[...] += dot(down_ref[...], act, 0, 0)
    gn2_ref[...] += dot(up_ref[...], grad_pre)
    gdown_ref[...] = dot(act, grad, 1, 1).astype(BF16)
    gup_ref[...] = dot(n2, grad_pre, 1, 1).astype(BF16)

    @pl.when(step == last)
    def _():
        hidden = hidden_ref[...]
        block_ref[...] = (hidden + out_ref[...]).T.astype(BF16)
        inv = lax.rsqrt(jnp.mean(hidden * hidden, axis=0, keepdims=True) + EPSILON)
        unit = hidden * inv
        gn2 = gn2_ref[...]
        ggain_ref[...] = jnp.broadcast_to(
            jnp.sum(gn2 * unit, axis=1, keepdims=True), ggain_ref.shape
        )
        a = gn2 * gain
        grad_hidden = gt_ref[...].astype(F32) + inv * (
            a - unit * jnp.mean(a * unit, axis=0, keepdims=True)
        )
        gh_ref[...] = grad_hidden
        branch = grad_hidden.astype(BF16)
        gwo_ref[...] = dot(mixed_ref[...], branch, 1, 1).astype(BF16)
        grad_mixed = dot(wo_ref[...], branch)
        rounded = grad_mixed.astype(BF16)
        dm_ref[...] = rounded
        size = width // heads
        rounded = rounded.astype(F32)
        for head in range(heads):
            rows_h = slice(head * size, (head + 1) * size)
            ctx, rec = ctx_ref[rows_h, :], rec_ref[rows_h, :]
            dc = jnp.sum(rounded[rows_h] * ctx, axis=0, keepdims=True)
            dn = jnp.sum(rounded[rows_h] * rec, axis=0, keepdims=True)
            dc_ref[head : head + 1, :] = dc
            dn_ref[head : head + 1, :] = dn
            share = gate_ref[head : head + 1, :]
            moved = jnp.sum(grad_mixed[rows_h] * (rec - ctx), axis=0, keepdims=True)
            dlogit_ref[head : head + 1, :] = moved * share * (1.0 - share)


def attend_back_kernel(
    lengths_ref, q_ref, k_ref, v_ref, mk_ref, mv_ref, dm_ref, gate_ref, bias_ref,
    lse_ref, lsen_ref, dc_ref, dn_ref,
    dq_ref, dk_ref, dv_ref, dmk_ref, dmv_ref,
    *, seg_count, scale,
):
    head = pl.program_id(0)
    size, rows = q_ref.shape
    seg_len = rows // seg_count
    penalty = local_penalty(lengths_ref, rows, seg_count)
    causal = causal_bias(TILE)
    q = q_ref[...].astype(F32) * (scale * LOG2E)
    q_high = q.astype(BF16)
    q_low = (q - q_high.astype(F32)).astype(BF16)
    row = pl.ds(head, 1)
    share = gate_ref[row, :]
    shift = jnp.log2(jnp.maximum(1.0 - share, 2.0**-60)) - lse_ref[row, :]
    near_shift = jnp.log2(jnp.maximum(share, 2.0**-60)) - lsen_ref[row, :] - shift
    dc = dc_ref[row, :]
    apart = dc - dn_ref[row, :]
    ones = jnp.ones((1, rows), F32)
    mem_ones = jnp.ones((1, mk_ref.shape[1]), F32)
    mem_three = pick_rows([mem_ones] * 3, 16).astype(BF16)
    queries = jnp.concatenate(
        [q_high, q_low, pick_rows([*three_parts(shift), ones], 16).astype(BF16)], axis=0
    )
    keys = jnp.concatenate(
        [k_ref[...], k_ref[...], pick_rows([ones, ones, ones, penalty], 16).astype(BF16)], axis=0
    )
    mem_keys = jnp.concatenate([mk_ref[...], mk_ref[...], mem_three], axis=0)
    grads = jnp.concatenate([dm_ref[...], pick_rows(three_parts(-dc), 16).astype(BF16)], axis=0)
    values = jnp.concatenate([v_ref[...], pick_rows([ones] * 3, 16).astype(BF16)], axis=0)
    mem_values = jnp.concatenate([mv_ref[...], mem_three], axis=0)
    for at in range(0, rows, TILE):
        here = slice(at, at + TILE)
        start = at // seg_len * seg_len
        q_here, dm_here = q_ref[:, here], dm_ref[:, here]
        score = dot(mem_keys, queries[:, here], 0, 0)
        moved = dot(mem_values, grads[:, here], 0, 0)
        far = jnp.exp2(score)
        near = jnp.exp2(score + (bias_ref[:, here] + near_shift[:, here]))
        weight = far + near
        dscore = (weight * moved + near * apart[:, here]).astype(BF16)
        grad_mv = dot(dm_here, weight.astype(BF16), 1, 1)
        grad_mk = dot(q_here, dscore, 1, 1)
        dq = dot(mk_ref[...], dscore)
        if at == 0:
            dmv_ref[...] = grad_mv
            dmk_ref[...] = grad_mk
        else:
            dmv_ref[...] += grad_mv
            dmk_ref[...] += grad_mk
        for block in range(start, at + TILE, TILE):
            there = slice(block, block + TILE)
            score = dot(keys[:, there], queries[:, here], 0, 0)
            if block == at:
                score = score + causal
            weight = jnp.exp2(score)
            dscore = (weight * dot(values[:, there], grads[:, here], 0, 0)).astype(BF16)
            grad_v = dot(dm_here, weight.astype(BF16), 1, 1)
            grad_k = dot(q_here, dscore, 1, 1)
            dq = dq + dot(k_ref[:, there], dscore)
            if block == at:
                dv_ref[:, there] = grad_v
                dk_ref[:, there] = grad_k
            else:
                dv_ref[:, there] += grad_v
                dk_ref[:, there] += grad_k
        dq_ref[:, here] = (scale * dq).astype(BF16)
    dk_ref[...] *= scale
    dmk_ref[...] *= scale


def weight_kernel(
    nt_ref, memory_ref, dq_ref, dk_ref, dv_ref, dmk_ref, dmv_ref, dlogit_ref, gw_ref, back_ref
):
    width = nt_ref.shape[0]
    normed = nt_ref[...]
    back_ref[0:width, :] = dq_ref[...]
    back_ref[width : 2 * width, :] = dk_ref[...].astype(BF16)
    back_ref[2 * width : 3 * width, :] = dv_ref[...].astype(BF16)
    for part in range(3):
        grad = dot(normed, back_ref[part * width : (part + 1) * width, :], 1, 1)
        if part:
            source = (dmk_ref, dmv_ref)[part - 1][...]
            high = source.astype(BF16)
            low = (source - high.astype(F32)).astype(BF16)
            grad = grad + dot(memory_ref[...], high, 0, 1) + dot(memory_ref[...], low, 0, 1)
        gw_ref[:, part * width : (part + 1) * width] = grad.astype(BF16)
    side = jnp.concatenate([dlogit_ref[...], jnp.zeros((SIDE - 8, nt_ref.shape[1]), F32)], axis=0)
    back_ref[3 * width :, :] = side.astype(BF16)


def input_kernel(
    xt_ref, inv_ref, nt_ref, w_ref, back_ref, gh_ref, ggain_ref, gx_ref, side_ref
):
    width = xt_ref.shape[0]
    unit = xt_ref[...].astype(F32) * inv_ref[0:1, :]
    side = w_ref[:, 3 * width :].astype(F32)
    gain = side[:, 8:9]
    grad = dot(w_ref[...], back_ref[...])
    gain_grad = jnp.sum(grad * unit, axis=1, keepdims=True)
    b = grad * gain
    out = gh_ref[...] + inv_ref[0:1, :] * (b - unit * jnp.mean(b * unit, axis=0, keepdims=True))
    gx_ref[...] = out.T
    gate_grad = dot(nt_ref[...], back_ref[3 * width :, :], 1, 1)
    lane = lax.broadcasted_iota(jnp.int32, gate_grad.shape, 1)
    gate_grad = jnp.where(lane == 8, gain_grad, gate_grad)
    side_ref[...] = jnp.where(lane == 9, ggain_ref[...], gate_grad).astype(BF16)


def on_device(
    tokens,
    memory,
    lengths,
    neighbours,
    out_grad,
    gain_one,
    gain_two,
    w_query,
    w_key,
    w_value,
    w_gate,
    w_out,
    w_up,
    w_down,
    *,
    sizes,
):
    rows, width = tokens.shape
    heads = w_gate.shape[1]
    size = width // heads
    seg_count = lengths.shape[0]
    knn = neighbours.shape[1]
    shard = w_query.shape[0]
    devices = sizes["dp"] * sizes["seq"]
    ff = w_up.shape[1]
    scale = size ** (-0.5)

    steps = gather_steps(sizes)
    place = places(steps, sizes)
    packed = jnp.concatenate(
        [
            w_query,
            w_key,
            w_value,
            w_gate,
            gain_one[:, None],
            gain_two[:, None],
            jnp.zeros((shard, SIDE - heads - 2), BF16),
        ],
        axis=1,
    )
    columns = packed.shape[1]
    w_in = jnp.take(doubled(packed[None], steps, sizes), place, axis=0).reshape(width, columns)
    seq_steps = [("seq", bit) for bit in reversed(bits_of(sizes["seq"]))]
    mem_all = doubled(memory[None], seq_steps, sizes).reshape(-1, width)
    slots = mem_all.shape[0]
    up_full = lax.all_gather(jnp.concatenate([w_out, w_up], axis=1), ("dp", "seq"), axis=0, tiled=True)
    out_full = up_full[:, :width]
    up_full = up_full[:, width:]
    down_full = lax.all_gather(w_down, ("dp", "seq"), axis=0, tiled=True)

    own = memory.shape[0]
    owner = (neighbours // own) ^ lax.axis_index("seq")
    ids = neighbours % own
    for at, (_, bit) in enumerate(seq_steps):
        ids = ids + jnp.where((owner & bit) != 0, own << at, 0)
    ids = jnp.pad(ids.T, ((0, 8 - knn), (0, 0)))

    big = (width, rows)
    rowsz = (8, rows)
    xt, gt, inv_one, bias = call(
        functools.partial(prepare_kernel, count=knn),
        [(big, BF16), (big, BF16), (rowsz, F32), ((slots, rows), F32)],
    )(tokens, out_grad, ids)

    nt, qkv, mem_kv, gate = call(
        project_kernel,
        [(big, BF16), ((3 * width, rows), BF16), ((2 * width, slots), BF16), (rowsz, F32)],
        flops=2 * width * rows * columns,
    )(xt, inv_one, w_in, mem_all)

    def head_block(part, cols):
        return pl.BlockSpec((size, cols), lambda h, *_: (part * heads + h, 0))

    smem = pl.BlockSpec(memory_space=pltpu.SMEM)
    mixed, ctx, rec, lse, lsen = call(
        functools.partial(attend_kernel, seg_count=seg_count, scale=scale),
        [(big, BF16), (big, F32), (big, F32), (rowsz, F32), (rowsz, F32)],
        grid=(heads,),
        in_specs=[
            smem,
            head_block(0, rows),
            head_block(1, rows),
            head_block(2, rows),
            head_block(0, slots),
            head_block(1, slots),
            whole(rowsz),
            whole((slots, rows)),
        ],
        out_specs=[head_block(0, rows)] * 3 + [whole(rowsz)] * 2,
        flops=8 * width * rows * (slots + rows),
    )(lengths, qkv, qkv, qkv, mem_kv, mem_kv, gate, bias)

    chunks = ff // width
    (
        block_out,
        grad_hidden,
        dm,
        dc,
        dn,
        dlogit,
        ggain_two,
        gwo,
        gup,
        gdown,
    ) = call(
        functools.partial(feed_kernel, heads=heads),
        [
            ((rows, width), BF16),
            (big, F32),
            (big, BF16),
            (rowsz, F32),
            (rowsz, F32),
            (rowsz, F32),
            ((width, SIDE), F32),
            ((width, width), BF16),
            ((width, ff), BF16),
            ((ff, width), BF16),
        ],
        grid=(chunks,),
        in_specs=[
            whole(big),
            whole(big),
            whole(big),
            whole(big),
            whole(big),
            whole(rowsz),
            pl.BlockSpec((width, SIDE), lambda c: (0, 3 * width // SIDE)),
            whole((width, width)),
            pl.BlockSpec((width, width), lambda c: (0, c)),
            pl.BlockSpec((width, width), lambda c: (c, 0)),
        ],
        out_specs=[
            whole((rows, width)),
            whole(big),
            whole(big),
            whole(rowsz),
            whole(rowsz),
            whole(rowsz),
            whole((width, SIDE)),
            whole((width, width)),
            pl.BlockSpec((width, width), lambda c: (0, c)),
            pl.BlockSpec((width, width), lambda c: (c, 0)),
        ],
        scratch=[
            pltpu.VMEM(big, F32),
            pltpu.VMEM(big, BF16),
            pltpu.VMEM(big, F32),
            pltpu.VMEM(big, F32),
        ],
        flops=12 * width * rows * ff,
    )(xt, gt, mixed, ctx, rec, gate, w_in, out_full, up_full, down_full)

    order = owners(steps, sizes)

    def to_owners(grad):
        return jnp.take(grad.reshape(devices, -1, grad.shape[1]), order, axis=0)

    late = jnp.concatenate(
        [
            to_owners(gdown),
            to_owners(gwo),
            *[to_owners(gup[:, c * width : (c + 1) * width]) for c in range(chunks)],
        ],
        axis=1,
    )
    late = halved(late, steps, sizes)

    dq, dk, dv, dmk, dmv = call(
        functools.partial(attend_back_kernel, seg_count=seg_count, scale=scale),
        [(big, BF16), (big, F32), (big, F32), ((width, slots), F32), ((width, slots), F32)],
        grid=(heads,),
        in_specs=[
            smem,
            head_block(0, rows),
            head_block(1, rows),
            head_block(2, rows),
            head_block(0, slots),
            head_block(1, slots),
            head_block(0, rows),
            whole(rowsz),
            whole((slots, rows)),
            whole(rowsz),
            whole(rowsz),
            whole(rowsz),
            whole(rowsz),
        ],
        out_specs=[head_block(0, rows)] * 3 + [head_block(0, slots)] * 2,
        flops=20 * width * rows * (slots + rows),
    )(lengths, qkv, qkv, qkv, mem_kv, mem_kv, dm, gate, bias, lse, lsen, dc, dn)

    gw, back = call(
        weight_kernel,
        [((width, 3 * width), BF16), ((3 * width + SIDE, rows), BF16)],
        flops=8 * width * rows * 3 * width,
    )(nt, mem_all, dq, dk, dv, dmk, dmv, dlogit)
    grad_tokens, side = call(
        input_kernel,
        [((rows, width), F32), ((width, SIDE), BF16)],
        flops=2 * width * rows * columns,
    )(xt, inv_one, nt, w_in, back, grad_hidden, ggain_two)

    early = halved(to_owners(jnp.concatenate([gw, side], axis=1)), steps, sizes)
    per_down = w_down.shape[0]
    grad_up = jnp.concatenate(
        [
            late[per_down + shard * (1 + c) : per_down + shard * (2 + c)]
            for c in range(chunks)
        ],
        axis=1,
    )
    side = early[:, 3 * width :]
    return (
        block_out,
        grad_tokens,
        side[:, heads],
        side[:, heads + 1],
        early[:, :width],
        early[:, width : 2 * width],
        early[:, 2 * width : 3 * width],
        side[:, :heads],
        late[per_down : per_down + shard],
        grad_up,
        late[:per_down],
    )


def solution(mesh):
    row_split, vector = P(("dp", "seq"), None), P(("dp", "seq"))
    in_specs = (row_split, row_split, vector, row_split, row_split, vector, vector) + (row_split,) * 7
    out_specs = (row_split, row_split, vector, vector) + (row_split,) * 7
    return jax.shard_map(
        functools.partial(on_device, sizes=dict(mesh.shape)),
        mesh=mesh,
        in_specs=in_specs,
        out_specs=out_specs,
        check_vma=False,
    )
```

time: 1770 us -> 317 us (0.18)
  waiting for transfers between devices: 858 us -> 111 us
  blocking collectives: 280 us -> 0 us
  matrix products: 258 us -> 0 us
  other arithmetic: 172 us -> 11.7 us
  local copies, waits for them, and re-layouts: 176 us -> 30.9 us
  Pallas kernels: 0 us -> 129 us
  starting transfers between devices: 0.74 us -> 19.5 us
    reduce_scatter x8 -> x0, waiting for transfers between devices: 812 us -> none  [the longest x1 140 us: reduce_grads(): lax.psum_scatter(terms[8], ('dp', 'seq'), scatter_dimension=0, tiled=True)]
    dot_general x136 -> x0, matrix products: 257 us -> none  [the longest x16 29.6 us: head_scores(): jnp.einsum('sqd,skd->sqk', query_h, key_h, preferred_element_type=jnp.flo...]
    all_gather x5 -> x0, blocking collectives: 206 us -> none  [the longest x1 45 us: fetch_weights(): lax.all_gather(shards[3], ('dp', 'seq'), axis=0, tiled=True)]
    pallas_call x0 -> x7, Pallas kernels: none -> 129 us  [the longest x1 39 us: on_device(): call(functools.partial(attend_back_kernel, seg_count=seg_count, scale=sca...]
    ppermute x0 -> x17, waiting for transfers between devices: none -> 76.1 us  [swap(): return lax.ppermute(array, axis, [(i, i ^ bit) for i in range(sizes[axis])])]
    unnamed x2 -> x0, blocking collectives: 74.2 us -> none
    scatter-add x2 -> x0, other arithmetic: 51.9 us -> none  [the longest x1 26 us: on_device(): jax.ops.segment_sum(grad_near_keys.reshape(rows * knn_count, width), flat...]
    unnamed x14 -> x2, waiting for transfers between devices: 46.1 us -> 0.03 us
  transfers between devices with their start and end apart: 13 -> 19, of which waited for: 7 -> 12; matrix products, arithmetic and copies ran while one was open for 20% -> 8% of each run, Pallas kernels for 0% -> 32%
where the time goes in v1:
time: 317 us
  Pallas kernels  129 us (41%)
  waiting for transfers between devices  111 us (35%)
  local copies, waits for them, and re-layouts  30.9 us (10%)
  starting transfers between devices  19.5 us (6%)
  between operations  14.4 us (5%)
  other arithmetic  11.7 us (4%)
    ppermute x17, waiting for transfers between devices, swap(): return lax.ppermute(array, axis, [(i, i ^ bit) for i in range(sizes[axis])])  76.1 us
    pallas_call x1, Pallas kernels, on_device(): call(functools.partial(attend_back_kernel, seg_count=seg_count, scale=sca...  39 us
    all_gather x1, waiting for transfers between devices, on_device(): down_full = lax.all_gather(w_down, ('dp', 'seq'), axis=0, tiled=True)  34.8 us
    pallas_call x1, Pallas kernels, on_device(): call(functools.partial(attend_kernel, seg_count=seg_count, scale=scale),...  31.3 us
    pallas_call x1, Pallas kernels, on_device(): call(functools.partial(feed_kernel, heads=heads), [((rows, width), BF16),...  27 us
    ppermute x17, starting transfers between devices, swap(): return lax.ppermute(array, axis, [(i, i ^ bit) for i in range(sizes[axis])])  19.4 us
    pallas_call x1, Pallas kernels, on_device(): call(weight_kernel, [((width, 3 * width), BF16), ((3 * width + SIDE, rows...  10.6 us
    gather x7, local copies, waits for them, and re-layouts, to_owners(): return jnp.take(grad.reshape(devices, -1, grad.shape[1]), order, axis=0)  8.38 us
  transfers between devices with their start and end apart: 19, of which 12 were waited for; matrix products, arithmetic and copies ran while one was open for 8% of the time, Pallas kernels for 32%

profile of v1, /device:TPU:0, one launch (start us, length us, event | category | flops | bytes accessed | tf_op | source)
XLA Modules:
  0.0 316.7 jit_solution(3032494630753668073)
XLA Ops:
  11.9 4.1 %collective-permute-start = (bf16[1,16,1664]{2,1,0:T(8,128)(2,1)S(1)}, bf16[1,16,1664]{2,1,0:T(8,128)(2,1)S(1)}, u32[]{:S(2)}, u32[]{:S(2)}) collective-permute-start(bf16[1,16,1664]{2,1,0:T(8,128)(2,1)S(1)} %bitcast.42), channel_id=1, source_target_pairs={{0,16},{4,20},{8,24},{12,28},{16,0},{20,4},{24,8},{28,12},{1,17},{... | collective-permute-start | bytes 159752 | tf_op jit(solution)/shard_map/ppermute | solution.py:75
  20.7 2.7 collective-permute-done.1
  23.5 1.8 collective-permute-start.2
  25.9 3.5 %collective-permute-done.2 = bf16[4,16,1664]{2,1,0:T(8,128)(2,1)S(1)} collective-permute-done((bf16[4,16,1664]{2,1,0:T(8,128)(2,1)S(1)}, bf16[4,16,1664]{2,1,0:T(8,128)(2,1)S(1)}, u32[]{:S(2)}, u32[]{:S(2)}) %collective-permute-start.2) | collective-permute-done | bytes 213024 | tf_op jit(solution)/shard_map/ppermute | solution.py:75
  29.5 1.8 collective-permute-start.3
  32.6 6.0 %collective-permute-done.3 = bf16[8,16,1664]{2,1,0:T(8,128)(2,1)S(1)} collective-permute-done((bf16[8,16,1664]{2,1,0:T(8,128)(2,1)S(1)}, bf16[8,16,1664]{2,1,0:T(8,128)(2,1)S(1)}, u32[]{:S(2)}, u32[]{:S(2)}) %collective-permute-start.3) | collective-permute-done | bytes 426016 | tf_op jit(solution)/shard_map/ppermute | solution.py:75
  40.1 6.8 %shard_map.221 = (bf16[512,1024]{1,0:T(8,128)(2,1)}, bf16[512,1024]{1,0:T(8,128)(2,1)}, f32[8,1024]{1,0:T(8,128)}, f32[1024,1024]{1,0:T(8,128)}) custom-call(bf16[1024,512]{1,0:T(8,128)(2,1)} %x_ref.1, bf16[1024,512]{1,0:T(8,128)(2,1)} %g_ref.1, s32[8,1024]{1,0:T(8,128)} %pad.4.ids_ref), custom_call_target="tpu_custom_call" | custom-call | tf_op jit(solution)/shard_map/pallas_call | solution.py:458
  52.6 6.6 %shard_map.222 = (bf16[512,1024]{1,0:T(8,128)(2,1)}, bf16[1536,1024]{1,0:T(8,128)(2,1)}, bf16[1024,1024]{1,0:T(8,128)(2,1)}, f32[8,1024]{1,0:T(8,128)}) custom-call(bf16[512,1024]{1,0:T(8,128)(2,1)} %get-tuple-element.45.xt_ref, f32[8,1024]{1,0:T(8,128)} %get-tuple-element.47.inv_ref, bf16[512,1664]{1,0:T(8,128)(2,1)} %bitcast.33, bf16[1024,512]{1,0:T(8,128)(2,1)} %bitcast.46), custom_call_target="tpu_custom_call" | custom-call | flops 1744830464 | tf_op jit(solution)/shard_map/pallas_call | solution.py:463
  59.2 31.3 %shard_map.223 = (bf16[512,1024]{1,0:T(8,128)(2,1)}, f32[512,1024]{1,0:T(8,128)}, f32[512,1024]{1,0:T(8,128)}, f32[8,1024]{1,0:T(8,128)}, f32[8,1024]{1,0:T(8,128)}) custom-call(s32[2]{0:T(128)} %lengths_ref.3, bf16[1536,1024]{1,0:T(8,128)(2,1)} %get-tuple-element.48.q_ref.k_ref.v_ref, bf16[1536,1024]{1,0:T(8,128)(2,1)} %get-tuple-element.48.q_ref.k_ref.v_ref, ...), custom_call_target="tpu_custom_call" | custom-call | flops 8589934592 | tf_op jit(solution)/shard_map/pallas_call | solution.py:473
  90.5 3.2 %slice.197.up_ref = bf16[512,2048]{1,0:T(8,128)(2,1)} slice(bf16[512,2560]{1,0:T(8,128)(2,1)} %all-gather.3.cloned.1.call-done), slice={[0:512], [512:2560]} | slice | bytes 4194304 | tf_op jit(solution)/shard_map/slice | solution.py:446
  93.7 1.9 slice.196.wo_ref
  95.6 34.8 %all-gather.5.cloned.1.call-done.down_ref = bf16[2048,512]{1,0:T(8,128)(2,1)} async-done(((bf16[64,512]{1,0:T(8,128)(2,1)}), bf16[2048,512]{1,0:T(8,128)(2,1)}) %all-gather.5.cloned.1.call-update) | async-done | bytes 2097168 | tf_op jit(solution)/shard_map/all_gather | solution.py:447
  130.4 27.0 %shard_map.224 = (bf16[1024,512]{1,0:T(8,128)(2,1)}, f32[512,1024]{1,0:T(8,128)}, bf16[512,1024]{1,0:T(8,128)(2,1)}, f32[8,1024]{1,0:T(8,128)}, f32[8,1024]{1,0:...) custom-call(bf16[512,1024]{1,0:T(8,128)(2,1)} %get-tuple-element.45., ...), custom_call_target="tpu_custom_call" | custom-call | flops 12884901888 | tf_op jit(solution)/shard_map/pallas_call | solution.py:503
  164.5 2.3 gather_fusion
  172.6 39.0 %shard_map.225 = (bf16[512,1024]{1,0:T(8,128)(2,1)}, f32[512,1024]{1,0:T(8,128)}, f32[512,1024]{1,0:T(8,128)}, f32[512,1024]{1,0:T(8,128)}, f32[512,1024]{1,0:T(8,128)}) custom-call(s32[2]{0:T(128)} %lengths_ref.3, bf16[1536,1024]{1,0:T(8,128)(2,1)} %get-tuple-element.48.q_ref.k_ref.v_ref, bf16[1536,1024]{1,0:T(8,128)(2,1)} %get-tuple-element.48.q_ref.k_ref.v_ref, ...), custom_call_target="tpu_custom_call" | custom-call | flops 21474836480 | tf_op jit(solution)/shard_map/pallas_call | solution.py:566
  211.5 10.6 %shard_map.226 = (bf16[512,1536]{1,0:T(8,128)(2,1)}, bf16[1664,1024]{1,0:T(8,128)(2,1)}) custom-call(bf16[512,1024]{1,0:T(8,128)(2,1)} %get-tuple-element.56.nt_ref, bf16[1024,512]{1,0:T(8,128)(2,1)} %bitcast.47, bf16[512,1024]{1,0:T(8,128)(2,1)} %get-tuple-element.62.dq_ref, f32[512,1024]{1,0:T(8,128)} %get-tuple-element.63.dk_ref, ...), custom_call_target="tpu_custom_call" | custom-call | flops 6442450944 | tf_op jit(solution)/shard_map/pallas_call | solution.py:589
  222.1 7.8 %shard_map.227 = (f32[1024,512]{1,0:T(8,128)}, bf16[512,128]{1,0:T(8,128)(2,1)}) custom-call(bf16[512,1024]{1,0:T(8,128)(2,1)} %get-tuple-element.45.xt_ref, f32[8,1024]{1,0:T(8,128)} %get-tuple-element.47.inv_ref, bf16[512,1024]{1,0:T(8,128)(2,1)} %get-tuple-element.56.nt_ref, bf16[512,1664]{1,0:T(8,128)(2,1)} %bitcast.35, ...), custom_call_target="tpu_custom_call" | custom-call | flops 1744830464 | tf_op jit(solution)/shard_map/pallas_call | solution.py:594
  232.4 3.1 add_convert_fusion
  238.1 34.9 %collective-permute-done.8 = bf16[8,16,1664]{2,1,0:T(8,128)(2,1)S(1)} collective-permute-done((bf16[8,16,1664]{2,1,0:T(8,128)(2,1)S(1)}, bf16[8,16,1664]{2,1,0:T(8,128)(2,1)S(1)}, u32[]{:S(2)}, u32[]{:S(2)}) %collective-permute-start.8) | collective-permute-done | bytes 426016 | tf_op jit(solution)/shard_map/ppermute | solution.py:75
  275.7 5.7 %collective-permute-done.9 = bf16[4,16,1664]{2,1,0:T(8,128)(2,1)S(1)} collective-permute-done((bf16[4,16,1664]{2,1,0:T(8,128)(2,1)S(1)}, bf16[4,16,1664]{2,1,0:T(8,128)(2,1)S(1)}, u32[]{:S(2)}, u32[]{:S(2)}) %collective-permute-start.9) | collective-permute-done | bytes 213024 | tf_op jit(solution)/shard_map/ppermute | solution.py:75
  282.1 4.4 %collective-permute-done.10 = bf16[2,16,1664]{2,1,0:T(8,128)(2,1)S(1)} collective-permute-done((bf16[2,16,1664]{2,1,0:T(8,128)(2,1)S(1)}, bf16[2,16,1664]{2,1,0:T(8,128)(2,1)S(1)}, u32[]{:S(2)}, u32[]{:S(2)}) %collective-permute-start.10) | collective-permute-done | bytes 106528 | tf_op jit(solution)/shard_map/ppermute | solution.py:75
  287.8 4.7 %collective-permute-done.14 = bf16[4,144,512]{2,1,0:T(8,128)(2,1)S(1)} collective-permute-done((bf16[4,144,512]{2,1,0:T(8,128)(2,1)S(1)}, bf16[4,144,512]{2,1,0:T(8,128)(2,1)S(1)}, u32[]{:S(2)}, u32[]{:S(2)}) %collective-permute-start.14) | collective-permute-done | bytes 589856 | tf_op jit(solution)/shard_map/ppermute | solution.py:75
  293.2 6.9 %collective-permute-done.15 = bf16[2,144,512]{2,1,0:T(8,128)(2,1)S(1)} collective-permute-done((bf16[2,144,512]{2,1,0:T(8,128)(2,1)S(1)}, bf16[2,144,512]{2,1,0:T(8,128)(2,1)S(1)}, u32[]{:S(2)}, u32[]{:S(2)}) %collective-permute-start.15) | collective-permute-done | bytes 294944 | tf_op jit(solution)/shard_map/ppermute | solution.py:75
  303.2 4.6 %collective-permute-done.16 = bf16[1,144,512]{2,1,0:T(8,128)(2,1)S(1)} collective-permute-done((bf16[1,144,512]{2,1,0:T(8,128)(2,1)S(1)}, bf16[1,144,512]{2,1,0:T(8,128)(2,1)S(1)}, u32[]{:S(2)}, u32[]{:S(2)}) %collective-permute-start.16) | collective-permute-done | bytes 147488 | tf_op jit(solution)/shard_map/ppermute | solution.py:75
  (110 shorter events, 46.7 us)
Async XLA Ops:
  7.2 83.3 %all-gather.3.cloned.1.call-start = ((), (), s32[]{:S(2)}) async-start(), calls=%async_computation | async-start | bytes 2703360 | tf_op jit(solution)/shard_map/all_gather | solution.py:444
  8.7 121.6 %all-gather.5.cloned.1.call-start = ((), (), s32[]{:S(2)}) async-start(), calls=%async_computation.1 | async-start | bytes 2162688 | tf_op jit(solution)/shard_map/all_gather | solution.py:447
  11.9 27.6 %copy-start.7 = (s32[1024,4]{0,1:T(4,128)S(1)}, s32[1024,4]{0,1:T(4,128)}, u32[]{:S(2)}) copy-start(s32[1024,4]{0,1:T(4,128)} %param.21) | copy-start | bytes 49156
  11.9 6.8 %collective-permute-start = (bf16[1,16,1664]{2,1,0:T(8,128)(2,1)S(1)}, bf16[1,16,1664]{2,1,0:T(8,128)(2,1)S(1)}, u32[]{:S(2)}, u32[]{:S(2)}) collective-permute-start(bf16[1,16,1664]{2,1,0:T(8,128)(2,1)S(1)} %bitcast.42), channel_id=1, source_target_pairs={{0,16},{4,20},{8,24},{12,28},{16,0},{20,4},{24,8},{28,12},{1,17},{... | collective-permute-start | bytes 159752 | tf_op jit(solution)/shard_map/ppermute | solution.py:75
  16.0 30.9 %collective-permute-start.5 = (bf16[1,256,512]{2,1,0:T(8,128)(2,1)}, bf16[1,256,512]{2,1,0:T(8,128)(2,1)S(1)}, u32[]{:S(2)}, u32[]{:S(2)}) collective-permute-start(bf16[1,256,512]{2,1,0:T(8,128)(2,1)} %bitcast.48), channel_id=1, source_target_pairs={{0,2},{1,3},{2,0},{3,1},{4,6},{5,7},{6,4},{7,5},{8,10},{9,11},{10,... | collective-permute-start | bytes 786440 | tf_op jit(solution)/shard_map/ppermute | solution.py:75
  18.7 4.8 %collective-permute-start.1 = (bf16[2,16,1664]{2,1,0:T(8,128)(2,1)S(1)}, bf16[2,16,1664]{2,1,0:T(8,128)(2,1)S(1)}, u32[]{:S(2)}, u32[]{:S(2)}) collective-permute-start(bf16[2,16,1664]{2,1,0:T(8,128)(2,1)S(1)} %pad_maximum_fusion.6), channel_id=1, source_target_pairs={{0,8},{4,12},{8,0},{12,4},{16,24},{20,28},{24,16},{28,20},{1,9},{5... | collective-permute-start | bytes 319496 | tf_op jit(solution)/shard_map/ppermute | solution.py:75
  23.5 5.9 %collective-permute-start.2 = (bf16[4,16,1664]{2,1,0:T(8,128)(2,1)S(1)}, bf16[4,16,1664]{2,1,0:T(8,128)(2,1)S(1)}, u32[]{:S(2)}, u32[]{:S(2)}) collective-permute-start(bf16[4,16,1664]{2,1,0:T(8,128)(2,1)S(1)} %pad_maximum_fusion.4), channel_id=1, source_target_pairs={{0,4},{4,0},{8,12},{12,8},{16,20},{20,16},{24,28},{28,24},{1,5},{5... | collective-permute-start | bytes 638984 | tf_op jit(solution)/shard_map/ppermute | solution.py:75
  29.5 9.2 %collective-permute-start.3 = (bf16[8,16,1664]{2,1,0:T(8,128)(2,1)S(1)}, bf16[8,16,1664]{2,1,0:T(8,128)(2,1)S(1)}, u32[]{:S(2)}, u32[]{:S(2)}) collective-permute-start(bf16[8,16,1664]{2,1,0:T(8,128)(2,1)S(1)} %pad_maximum_fusion.3), channel_id=1, source_target_pairs={{0,2},{1,3},{2,0},{3,1},{4,6},{5,7},{6,4},{7,5},{8,10},{9,11},{10,... | collective-permute-start | bytes 1277960 | tf_op jit(solution)/shard_map/ppermute | solution.py:75
  31.9 15.0 %copy-start.5 = (bf16[256,512]{1,0:T(8,128)(2,1)S(1)}, bf16[256,512]{1,0:T(8,128)(2,1)}, u32[]{:S(2)}) copy-start(bf16[256,512]{1,0:T(8,128)(2,1)} %param.19) | copy-start | bytes 786436
  39.4 10.7 %collective-permute-start.4 = (bf16[16,16,1664]{2,1,0:T(8,128)(2,1)}, bf16[16,16,1664]{2,1,0:T(8,128)(2,1)S(1)}, u32[]{:S(2)}, u32[]{:S(2)}) collective-permute-start(bf16[16,16,1664]{2,1,0:T(8,128)(2,1)} %get-tuple-element.120), channel_id=1, source_target_pairs={{0,1},{1,0},{2,3},{3,2},{4,5},{5,4},{6,7},{7,6},{8,9},{9,8},{10,11... | collective-permute-start | bytes 2555912 | tf_op jit(solution)/shard_map/ppermute | solution.py:75
  47.0 2.1 collective-permute-start.6
  157.4 1.7 copy-start.6
  169.4 2.9 copy-start
  172.3 60.2 %collective-permute-start.12 = (bf16[16,144,512]{2,1,0:T(8,128)(2,1)}, bf16[16,144,512]{2,1,0:T(8,128)(2,1)}, u32[]{:S(2)}, u32[]{:S(2)}) collective-permute-start(bf16[16,144,512]{2,1,0:T(8,128)(2,1)} %slice.215), channel_id=1, source_target_pairs={{0,1},{1,0},{2,3},{3,2},{4,5},{5,4},{6,7},{7,6},{8,9},{9,8},{10,11... | collective-permute-start | bytes 7077896 | tf_op jit(solution)/shard_map/ppermute | solution.py:75
  222.1 7.8 %copy-start.4 = (bf16[512,1536]{1,0:T(8,128)(2,1)S(1)}, bf16[512,1536]{1,0:T(8,128)(2,1)}, u32[]{:S(2)}) copy-start(bf16[512,1536]{1,0:T(8,128)(2,1)} %get-tuple-element.72) | copy-start | bytes 4718596
  232.1 5.0 %collective-permute-start.7 = (bf16[16,16,1664]{2,1,0:T(8,128)(2,1)S(1)}, bf16[16,16,1664]{2,1,0:T(8,128)(2,1)S(1)}, u32[]{:S(2)}, u32[]{:S(2)}) collective-permute-start(bf16[16,16,1664]{2,1,0:T(8,128)(2,1)S(1)} %slice.199), channel_id=1, source_target_pairs={{0,1},{1,0},{2,3},{3,2},{4,5},{5,4},{6,7},{7,6},{8,9},{9,8},{10,11... | collective-permute-start | bytes 2555912 | tf_op jit(solution)/shard_map/ppermute | solution.py:75
  235.7 39.0 %collective-permute-start.13 = (bf16[8,144,512]{2,1,0:T(8,128)(2,1)S(1)}, bf16[8,144,512]{2,1,0:T(8,128)(2,1)S(1)}, u32[]{:S(2)}, u32[]{:S(2)}) collective-permute-start(bf16[8,144,512]{2,1,0:T(8,128)(2,1)S(1)} %slice.217), channel_id=1, source_target_pairs={{0,2},{1,3},{2,0},{3,1},{4,6},{5,7},{6,4},{7,5},{8,10},{9,11},{10,... | collective-permute-start | bytes 3538952 | tf_op jit(solution)/shard_map/ppermute | solution.py:75
  237.4 35.6 %collective-permute-start.8 = (bf16[8,16,1664]{2,1,0:T(8,128)(2,1)S(1)}, bf16[8,16,1664]{2,1,0:T(8,128)(2,1)S(1)}, u32[]{:S(2)}, u32[]{:S(2)}) collective-permute-start(bf16[8,16,1664]{2,1,0:T(8,128)(2,1)S(1)} %slice.201), channel_id=1, source_target_pairs={{0,2},{1,3},{2,0},{3,1},{4,6},{5,7},{6,4},{7,5},{8,10},{9,11},{10,... | collective-permute-start | bytes 1277960 | tf_op jit(solution)/shard_map/ppermute | solution.py:75
  273.1 8.3 %collective-permute-start.9 = (bf16[4,16,1664]{2,1,0:T(8,128)(2,1)S(1)}, bf16[4,16,1664]{2,1,0:T(8,128)(2,1)S(1)}, u32[]{:S(2)}, u32[]{:S(2)}) collective-permute-start(bf16[4,16,1664]{2,1,0:T(8,128)(2,1)S(1)} %slice.203), channel_id=1, source_target_pairs={{0,4},{4,0},{8,12},{12,8},{16,20},{20,16},{24,28},{28,24},{1,5},{5... | collective-permute-start | bytes 638984 | tf_op jit(solution)/shard_map/ppermute | solution.py:75
  275.0 17.4 %collective-permute-start.14 = (bf16[4,144,512]{2,1,0:T(8,128)(2,1)S(1)}, bf16[4,144,512]{2,1,0:T(8,128)(2,1)S(1)}, u32[]{:S(2)}, u32[]{:S(2)}) collective-permute-start(bf16[4,144,512]{2,1,0:T(8,128)(2,1)S(1)} %slice.219), channel_id=1, source_target_pairs={{0,4},{4,0},{8,12},{12,8},{16,20},{20,16},{24,28},{28,24},{1,5},{5... | collective-permute-start | bytes 1769480 | tf_op jit(solution)/shard_map/ppermute | solution.py:75
  281.4 5.1 %collective-permute-start.10 = (bf16[2,16,1664]{2,1,0:T(8,128)(2,1)S(1)}, bf16[2,16,1664]{2,1,0:T(8,128)(2,1)S(1)}, u32[]{:S(2)}, u32[]{:S(2)}) collective-permute-start(bf16[2,16,1664]{2,1,0:T(8,128)(2,1)S(1)} %slice.205), channel_id=1, source_target_pairs={{0,8},{4,12},{8,0},{12,4},{16,24},{20,28},{24,16},{28,20},{1,9},{5... | collective-permute-start | bytes 319496 | tf_op jit(solution)/shard_map/ppermute | solution.py:75
  286.5 6.7 %collective-permute-start.11 = (bf16[1,16,1664]{2,1,0:T(8,128)(2,1)S(1)}, bf16[1,16,1664]{2,1,0:T(8,128)(2,1)S(1)}, u32[]{:S(2)}, u32[]{:S(2)}) collective-permute-start(bf16[1,16,1664]{2,1,0:T(8,128)(2,1)S(1)} %slice.207), channel_id=1, source_target_pairs={{0,16},{4,20},{8,24},{12,28},{16,0},{20,4},{24,8},{28,12},{1,17},{... | collective-permute-start | bytes 159752 | tf_op jit(solution)/shard_map/ppermute | solution.py:75
  292.6 7.5 %collective-permute-start.15 = (bf16[2,144,512]{2,1,0:T(8,128)(2,1)S(1)}, bf16[2,144,512]{2,1,0:T(8,128)(2,1)S(1)}, u32[]{:S(2)}, u32[]{:S(2)}) collective-permute-start(bf16[2,144,512]{2,1,0:T(8,128)(2,1)S(1)} %slice.221), channel_id=1, source_target_pairs={{0,8},{4,12},{8,0},{12,4},{16,24},{20,28},{24,16},{28,20},{1,9},{5... | collective-permute-start | bytes 884744 | tf_op jit(solution)/shard_map/ppermute | solution.py:75
  300.2 7.6 %collective-permute-start.16 = (bf16[1,144,512]{2,1,0:T(8,128)(2,1)S(1)}, bf16[1,144,512]{2,1,0:T(8,128)(2,1)S(1)}, u32[]{:S(2)}, u32[]{:S(2)}) collective-permute-start(bf16[1,144,512]{2,1,0:T(8,128)(2,1)S(1)} %slice.223), channel_id=1, source_target_pairs={{0,16},{4,20},{8,24},{12,28},{16,0},{20,4},{24,8},{28,12},{1,17},{... | collective-permute-start | bytes 442376 | tf_op jit(solution)/shard_map/ppermute | solution.py:75
  (3 other events, 3.3 us)
Sparse Core Ops, SparseCore 0:
  11.4 60.6 all-gather.2
  75.0 55.3 all-gather.4
